TPU v7x, 32 devices: a whole 2x2x4 slice. The times are simulated.
32 devices in a mesh: row: 8 (over z, y), col: 4 (over x, core).
Axes of the slice: x: 2, y: 2, z: 4, core: 2. Of those that a mesh axis runs over, the one named last changes fastest.
Arguments:
- trailing_inverse: bfloat16 [2048, 2048], P('row', 'col'), may hold values from -0.125 to 0.125
- l_panel: bfloat16 [2048, 512], P('row', 'col'), may hold values from -6 to 6
- pattern: int32 [8, 2], replicated, may hold values 0 or 1
Outputs:
- inverse_panel: float32 [2048, 512], P('row', 'col')
Inputs may be any that keep to these rules, and one draw needn't show every extreme that they name: pattern holds only 0 and 1.
All inputs are finite; a program needn't handle non-finite values.
Results may differ from a plain program's by a relative error of at most 0.0003.
Values may be sent and summed in bfloat16 or wider, within the bound.
A program may use at most 64 MiB of HBM per device.

v0:
```python
import jax
import jax.numpy as jnp
from jax import lax
from jax.sharding import PartitionSpec as P

B = 256
RB = 1


def broadcast(value, axis, source):
    kept = jnp.where(lax.axis_index(axis) == source, value, 0).astype(value.dtype)
    return lax.psum(kept, axis)


def per_device(trailing_inverse, l_panel, pattern):
    grid_row = lax.axis_index("row")
    grid_col = lax.axis_index("col")
    ratio = lax.axis_size("row") // lax.axis_size("col")
    local_rows = l_panel.shape[0]
    supernodes = pattern.shape[1]
    my_pattern = lax.dynamic_slice_in_dim(pattern, grid_row * RB, RB, 0)
    full_row = lax.all_gather(l_panel, "col", axis=1, tiled=True)
    keep = my_pattern.astype(jnp.bfloat16)
    masked_row = (full_row.reshape(RB, B, supernodes, B) * keep[:, None, :, None]).reshape(
        local_rows, supernodes * B
    )
    arrived = []
    columns = []
    for turn in range(ratio):
        root = grid_col * ratio + turn
        piece = broadcast(masked_row, "row", root)
        inverse_cols = lax.dynamic_slice_in_dim(trailing_inverse, turn * local_rows, local_rows, 1)
        arrived.append(piece)
        columns.append(inverse_cols)
    stacked_panel = jnp.concatenate(arrived, 0)
    stacked_inverse = jnp.concatenate(columns, 1)
    partial_value = jnp.dot(stacked_inverse, stacked_panel, preferred_element_type=jnp.float32)
    negated = -my_pattern.astype(jnp.float32)
    signed = (partial_value.reshape(RB, B, supernodes, B) * negated[:, None, :, None]).reshape(
        local_rows, supernodes * B
    )
    return lax.psum_scatter(signed, "col", scatter_dimension=1, tiled=True)


def solution(mesh):
    return jax.shard_map(
        per_device,
        mesh=mesh,
        in_specs=(P("row", "col"), P("row", "col"), P()),
        out_specs=P("row", "col"),
        check_vma=False,
    )
```

profile of v0, /device:TPU:0, one launch (start us, length us, event | category | flops | bytes accessed | tf_op | source)
XLA Modules:
  0.0 121.9 jit_solution(7141890469558297486)
XLA Ops:
  6.5 0.0 copy-start
  6.5 0.0 all-reduce.3.cloned.1.call-start
  6.5 0.0 copy-start.1
  6.5 0.7 copy-done.1
  7.3 0.2 fusion.4
  7.4 0.1 broadcast_bitcast_fusion.1
  7.5 7.4 %all_gather.3 = bf16[256,512]{1,0:T(8,128)(2,1)S(1)} all-gather(bf16[256,128]{1,0:T(8,128)(2,1)} %param.4), channel_id=1, replica_groups=mesh['row'=8,'col'=4] {'col'}, dimensions={1}, use_global_device_ids=true | all-gather | bytes 327680 | tf_op jit(solution)/shard_map/all_gather | solution.py:22
  14.9 0.8 broadcast_select_fusion.1
  15.8 0.0 all-reduce.3.cloned.1.call-update
  15.8 0.0 reduce-scatter.2.cloned.1.call-start
  15.8 0.2 negate_reduce_fusion
  16.0 0.1 broadcast_bitcast_fusion
  16.1 73.8 %all-reduce.3.cloned.1.call-done = (bf16[256,512]{1,0:T(8,128)(2,1)}, bf16[256,512]{1,0:T(8,128)(2,1)}) async-done(((bf16[256,512]{1,0:T(8,128)(2,1)}, bf16[256,512]{1,0:T(8,128)(2,1)}), (bf16[256,512]{1,0:T(8,128)(2,1)}, bf16[256,512]{1,0:T(8,128)(2,1)})) %all-reduce.3.cloned.1.call-update) | async-done | bytes 524304 | tf_op jit(solution)/shard_map/psum | solution.py:12
  89.9 0.0 copy-done
  89.9 2.2 %fusion = f32[256,512]{0,1:T(8,128)} fusion(bf16[256,512]{1,0:T(8,128)(2,1)S(1)} %copy-done, bf16[256,512]{1,0:T(8,128)(2,1)} %get-tuple-element.5, bf16[256,512]{1,0:T(8,128)(2,1)} %get-tuple-element.6, f32[512]{0:T(512)S(1)} %bitcast.10), kind=kOutput, calls=%fused_computation.1 | convolution fusion | flops 135397376 | bytes 1312768 | tf_op jit(solution)/shard_map/dot_general | solution.py:37
  92.1 0.0 reduce-scatter.2.cloned.1.call-update
  92.1 21.3 %reduce-scatter.2.cloned.1.call-done = f32[256,128]{0,1:T(8,128)} async-done(((f32[256,512]{0,1:T(8,128)}), f32[256,128]{0,1:T(8,128)}) %reduce-scatter.2.cloned.1.call-update) | async-done | bytes 131088 | tf_op jit(solution)/shard_map/reduce_scatter | solution.py:42
  113.4 1.7 %copy.4 = f32[256,128]{1,0:T(8,128)} copy(f32[256,128]{0,1:T(8,128)} %reduce-scatter.2.cloned.1.call-done) | data formatting | bytes 262144 | tf_op jit(solution)/shard_map/reduce_scatter | solution.py:42
  (2 shorter events, 0.0 us)
Async XLA Ops:
  6.5 83.4 %copy-start = (bf16[256,512]{1,0:T(8,128)(2,1)S(1)}, bf16[256,512]{1,0:T(8,128)(2,1)}, u32[]{:S(2)}) copy-start(bf16[256,512]{1,0:T(8,128)(2,1)} %param.3) | copy-start | bytes 786436
  6.5 83.4 %all-reduce.3.cloned.1.call-start = ((), (), s32[]{:S(2)}) async-start(), calls=%async_computation.2 | async-start | bytes 1048576 | tf_op jit(solution)/shard_map/psum | solution.py:12
  6.5 0.7 copy-start.1
  15.8 97.6 %reduce-scatter.2.cloned.1.call-start = ((), (), s32[]{:S(2)}) async-start(), calls=%async_computation.1 | async-start | bytes 655360 | tf_op jit(solution)/shard_map/reduce_scatter | solution.py:42
Sparse Core Ops, SparseCore 0:
  15.9 73.9 all-reduce.2
  92.6 20.8 reduce-scatter.1
where the time goes:
time: 122 us
  waiting for transfers between devices  95.2 us (78%)
  between operations  13.4 us (11%)
  blocking collectives  7.41 us (6%)
  local copies, waits for them, and re-layouts  2.54 us (2%)
  matrix products  2.17 us (2%)
    psum x1, waiting for transfers between devices, broadcast(): return lax.psum(kept, axis)  73.8 us
    reduce_scatter x1, waiting for transfers between devices, per_device(): return lax.psum_scatter(signed, 'col', scatter_dimension=1, tiled=True)  21.3 us
    all_gather x1, blocking collectives, per_device(): full_row = lax.all_gather(l_panel, 'col', axis=1, tiled=True)  7.41 us
  transfers between devices with their start and end apart: 2, of which 2 were waited for; matrix products, arithmetic and copies ran while one was open for 0% of the time, Pallas kernels for 0%

commit v1 on v0

--- a/solution.py
+++ b/solution.py
@@ -1,10 +1,17 @@
+import functools
+
 import jax
 import jax.numpy as jnp
 from jax import lax
+from jax.experimental import pallas as pl
+from jax.experimental.pallas import tpu as pltpu
 from jax.sharding import PartitionSpec as P
 
 B = 256
 RB = 1
+MESH = pl.DeviceIdType.MESH
+T_CHUNKS = 4
+P_CHUNKS = 2
 
 
 def broadcast(value, axis, source):
@@ -42,9 +49,202 @@
     return lax.psum_scatter(signed, "col", scatter_dimension=1, tiled=True)
 
 
+def kernel(pattern_ref, t_ref, l_ref, out_ref, t_own, t_far, l_own, l_masked, m, p_send, p_recv,
+           load_sem, z_send, c_send, f_send, t_send, t_recv, q_send, q_recv, m_recv):
+    row = lax.axis_index("row")
+    col = lax.axis_index("col")
+    z, y = row // 2, row % 2
+    x, k = col // 2, col % 2
+    home = z % 2
+    is_home = k == home
+    rel = (k + home) % 2
+    near = (z // 2 + x) % 2
+
+    def at(z_, y_, x_, k_):
+        return (z_ * 2 + y_, x_ * 2 + k_)
+
+    def slot(rel_, zrel_, y_):
+        rows = pl.ds(pl.multiple_of((zrel_ * 2 + y_) * B, B), B)
+        return m.at[rel_, rows], m_recv.at[(rel_ * 2 + zrel_) * 2 + y_]
+
+    def copy(src, dst, send, recv, where):
+        return pltpu.make_async_remote_copy(
+            src_ref=src, dst_ref=dst, send_sem=send, recv_sem=recv, device_id=where, device_id_type=MESH
+        )
+
+    x_mate = at(z, y, 1 - x, k)
+    sibling = at(z, y, x, 1 - k)
+    y_mate = at(z, 1 - y, x, k)
+
+    load_l = pltpu.make_async_copy(l_ref, l_own, load_sem.at[0])
+    load_t = pltpu.make_async_copy(t_ref, t_own, load_sem.at[1])
+    load_l.start()
+    load_t.start()
+
+    barrier = pltpu.get_barrier_semaphore()
+
+    def greet(where):
+        pl.semaphore_signal(barrier, inc=1, device_id=where, device_id_type=MESH)
+
+    greet(x_mate)
+    greet(sibling)
+    greet(y_mate)
+    for zi in range(2):
+        @pl.when(2 * zi + k != z)
+        def _(zi=zi):
+            greet(at(2 * zi + k, y, x, 0))
+            greet(at(2 * zi + k, y, x, 1))
+
+    @pl.when(is_home)
+    def _():
+        greet(at(z, 1 - y, x, 1 - k))
+
+    load_l.wait()
+    keep = pattern_ref[row, x].astype(jnp.float32)
+    l_masked[...] = (l_own[...].astype(jnp.float32) * keep).astype(jnp.bfloat16)
+
+    @pl.when(is_home)
+    def _():
+        rows = pl.ds(pl.multiple_of((near * 2 + y) * B, B), B)
+        m[0, rows, :] = l_masked[...]
+
+    @pl.when(is_home)
+    def _():
+        pl.semaphore_wait(barrier, 6)
+
+    @pl.when(jnp.logical_not(is_home))
+    def _():
+        pl.semaphore_wait(barrier, 7)
+
+    mine, mine_sem = slot(rel, near, y)
+    z_copies = [
+        copy(l_masked, mine, z_send.at[i], mine_sem, at(z_to, y, x, home))
+        for i, z_to in enumerate((3 - z, (z + 2) % 4, z + 1 - 2 * (z % 2)))
+    ]
+    cross = copy(l_masked, mine, c_send.at[0], mine_sem, at(z, 1 - y, x, home))
+    inside = copy(l_masked, mine, c_send.at[1], mine_sem, sibling)
+    t_rows = t_far.shape[0] // T_CHUNKS
+    t_copies = [
+        copy(t_ref.at[pl.ds(i * t_rows, t_rows)], t_far.at[pl.ds(i * t_rows, t_rows)],
+             t_send.at[i], t_recv.at[i], x_mate)
+        for i in range(T_CHUNKS)
+    ]
+    for c in z_copies:
+        c.start()
+    cross.start()
+
+    @pl.when(jnp.logical_not(is_home))
+    def _():
+        inside.start()
+
+    for c in t_copies:
+        c.start()
+
+    forwards = []
+    for step, zi in enumerate((z // 2, 1 - z // 2)):
+        zrel = (zi + x) % 2
+        from_afar = 2 * zi + k != z
+        for r in range(2):
+            block, sem = slot(r, zrel, y)
+            f = copy(block, block, f_send.at[step * 2 + r], sem, y_mate)
+            forwards.append((from_afar, f))
+
+            @pl.when(from_afar)
+            def _(f=f):
+                f.wait_recv()
+                f.start()
+
+    @pl.when(is_home)
+    def _():
+        block, sem = slot(1, near, y)
+        copy(block, block, c_send.at[1], sem, sibling).wait_recv()
+
+    for step, zi in enumerate((z // 2, 1 - z // 2)):
+        zrel = (zi + x) % 2
+        for r in range(2):
+            block, sem = slot(r, zrel, 1 - y)
+            copy(block, block, f_send.at[0], sem, y_mate).wait_recv()
+
+    load_t.wait()
+    for c in t_copies:
+        c.wait_recv()
+    depth = t_own.shape[1]
+    p_rows = out_ref.shape[0] // P_CHUNKS
+    swaps = []
+    near_m = jnp.concatenate([m[0, :depth, :], m[1, :depth, :]], axis=1)
+    far_m = jnp.concatenate([m[0, depth:, :], m[1, depth:, :]], axis=1)
+    for i in range(P_CHUNKS):
+        rows = pl.ds(i * p_rows, p_rows)
+        part = jnp.dot(t_own[rows, :], near_m, preferred_element_type=jnp.float32)
+        part += jnp.dot(t_far[rows, :], far_m, preferred_element_type=jnp.float32)
+        width = out_ref.shape[1]
+        p_send[rows, :] = part[:, width:]
+        s = copy(p_send.at[rows], p_recv.at[rows], q_send.at[i], q_recv.at[i], sibling)
+        s.start()
+        swaps.append(s)
+        out_ref[rows, :] = part[:, :width]
+    for i in range(P_CHUNKS):
+        rows = pl.ds(i * p_rows, p_rows)
+        swaps[i].wait_recv()
+        out_ref[rows, :] = (out_ref[rows, :] + p_recv[rows, :]) * -keep
+
+    for c in z_copies + [cross] + t_copies + swaps:
+        c.wait_send()
+
+    @pl.when(jnp.logical_not(is_home))
+    def _():
+        inside.wait_send()
+
+    for from_afar, f in forwards:
+        @pl.when(from_afar)
+        def _(f=f):
+            f.wait_send()
+
+
+def fused(trailing_inverse, l_panel, pattern):
+    rows, depth = trailing_inverse.shape
+    width = l_panel.shape[1]
+    planes = 2
+    return pl.pallas_call(
+        kernel,
+        out_shape=jax.ShapeDtypeStruct((rows, width), jnp.float32),
+        in_specs=[
+            pl.BlockSpec(memory_space=pltpu.SMEM),
+            pl.BlockSpec(memory_space=pl.ANY),
+            pl.BlockSpec(memory_space=pl.ANY),
+        ],
+        out_specs=pl.BlockSpec(memory_space=pltpu.VMEM),
+        scratch_shapes=[
+            pltpu.VMEM((rows, depth), jnp.bfloat16),
+            pltpu.VMEM((rows, depth), jnp.bfloat16),
+            pltpu.VMEM((B, width), jnp.bfloat16),
+            pltpu.VMEM((B, width), jnp.bfloat16),
+            pltpu.VMEM((2, planes * depth, width), jnp.bfloat16),
+            pltpu.VMEM((rows, width), jnp.float32),
+            pltpu.VMEM((rows, width), jnp.float32),
+            pltpu.SemaphoreType.DMA((2,)),
+            pltpu.SemaphoreType.DMA((3,)),
+            pltpu.SemaphoreType.DMA((2,)),
+            pltpu.SemaphoreType.DMA((4,)),
+            pltpu.SemaphoreType.DMA((T_CHUNKS,)),
+            pltpu.SemaphoreType.DMA((T_CHUNKS,)),
+            pltpu.SemaphoreType.DMA((P_CHUNKS,)),
+            pltpu.SemaphoreType.DMA((P_CHUNKS,)),
+            pltpu.SemaphoreType.DMA((8,)),
+        ],
+        compiler_params=pltpu.CompilerParams(
+            collective_id=0, has_side_effects=True, vmem_limit_bytes=16 * 1024 * 1024
+        ),
+        cost_estimate=pl.CostEstimate(
+            flops=2 * rows * planes * depth * 2 * width, bytes_accessed=rows * depth * 4, transcendentals=0
+        ),
+    )(pattern, trailing_inverse, l_panel)
+
+
 def solution(mesh):
+    whole_block = (mesh.shape["row"], mesh.shape["col"]) == (8, 4)
     return jax.shard_map(
-        per_device,
+        fused if whole_block else per_device,
         mesh=mesh,
         in_specs=(P("row", "col"), P("row", "col"), P()),
         out_specs=P("row", "col"),

time: 122 us -> 22.6 us (0.19)
  waiting for transfers between devices: 95.2 us -> 0 us
  Pallas kernels: 0 us -> 19.2 us
  between operations: 13.4 us -> 0.01 us
  blocking collectives: 7.41 us -> 0 us
  matrix products: 2.17 us -> 0 us
    psum x1 -> x0, waiting for transfers between devices: 73.8 us -> none  [broadcast(): return lax.psum(kept, axis)]
    reduce_scatter x1 -> x0, waiting for transfers between devices: 21.3 us -> none  [per_device(): return lax.psum_scatter(signed, 'col', scatter_dimension=1, tiled=True)]
    pallas_call x0 -> x1, Pallas kernels: none -> 19.2 us  [fused(): pl.pallas_call(kernel, out_shape=jax.ShapeDtypeStruct((rows, width), jnp....]
    all_gather x1 -> x0, blocking collectives: 7.41 us -> none  [per_device(): full_row = lax.all_gather(l_panel, 'col', axis=1, tiled=True)]
    unnamed x8 -> x6, local copies, waits for them, and re-layouts: 0.89 us -> 3.2 us
    dot_general x1 -> x0, matrix products: 2.17 us -> none  [per_device(): jnp.dot(stacked_inverse, stacked_panel, preferred_element_type=jnp.float32)]
    reduce_scatter x1 -> x0, local copies, waits for them, and re-layouts: 1.66 us -> none  [per_device(): return lax.psum_scatter(signed, 'col', scatter_dimension=1, tiled=True)]
  transfers between devices with their start and end apart: 2 -> 0, of which waited for: 2 -> 0; matrix products, arithmetic and copies ran while one was open for 0% -> 0% of each run, Pallas kernels for 0% -> 0%
where the time goes in v1:
time: 22.6 us; the launch traced here: 22.4 us
  Pallas kernels  19.2 us (85%)
  local copies, waits for them, and re-layouts  3.2 us (14%)
    pallas_call x1, Pallas kernels, fused(): pl.pallas_call(kernel, out_shape=jax.ShapeDtypeStruct((rows, width), jnp....  19.2 us
    unnamed x6, local copies, waits for them, and re-layouts  3.2 us

profile of v1, /device:TPU:0, one launch (start us, length us, event | category | flops | bytes accessed | tf_op | source)
XLA Modules:
  0.0 22.4 jit_solution(12056333064956873218)
XLA Ops:
  0.0 0.8 %copy.4.pattern_ref = s32[8,2]{1,0:T(8,128)S(1)} copy(s32[8,2]{0,1:T(2,128)} %param.5) | data formatting | bytes 128 | tf_op args[2]
  0.8 0.0 copy-start
  0.8 0.9 %copy-done = bf16[256,512]{1,0:T(8,128)(2,1)S(1)} copy-done((bf16[256,512]{1,0:T(8,128)(2,1)S(1)}, bf16[256,512]{1,0:T(8,128)(2,1)}, u32[]{:S(2)}) %copy-start) | copy-done | bytes 262168
  1.7 0.0 copy-start.1
  1.7 0.8 %copy-done.1 = bf16[256,128]{1,0:T(8,128)(2,1)S(1)} copy-done((bf16[256,128]{1,0:T(8,128)(2,1)S(1)}, bf16[256,128]{1,0:T(8,128)(2,1)}, u32[]{:S(2)}) %copy-start.1) | copy-done | bytes 65560
  2.5 19.2 %shard_map.37 = f32[256,128]{1,0:T(8,128)S(1)} custom-call(s32[8,2]{1,0:T(8,128)S(1)} %copy.4.pattern_ref, bf16[256,512]{1,0:T(8,128)(2,1)S(1)} %copy-done, bf16[256,128]{1,0:T(8,128)(2,1)S(1)} %copy-done.1), custom_call_target="tpu_custom_call" | custom-call | flops 134217728 | bytes 524288 | tf_op jit(solution)/shard_map/pallas_call | solution.py:208
  21.7 0.7 %copy.6 = f32[256,128]{1,0:T(8,128)} copy(f32[256,128]{1,0:T(8,128)S(1)} %shard_map.37) | data formatting | bytes 262144
Async XLA Ops:
  0.8 0.9 %copy-start = (bf16[256,512]{1,0:T(8,128)(2,1)S(1)}, bf16[256,512]{1,0:T(8,128)(2,1)}, u32[]{:S(2)}) copy-start(bf16[256,512]{1,0:T(8,128)(2,1)} %t_ref.1) | copy-start | bytes 786436
  1.7 0.8 %copy-start.1 = (bf16[256,128]{1,0:T(8,128)(2,1)S(1)}, bf16[256,128]{1,0:T(8,128)(2,1)}, u32[]{:S(2)}) copy-start(bf16[256,128]{1,0:T(8,128)(2,1)} %l_ref.1) | copy-start | bytes 196612

commit v2 on v0

--- a/solution.py
+++ b/solution.py
@@ -1,10 +1,17 @@
+import functools
+
 import jax
 import jax.numpy as jnp
 from jax import lax
+from jax.experimental import pallas as pl
+from jax.experimental.pallas import tpu as pltpu
 from jax.sharding import PartitionSpec as P
 
 B = 256
 RB = 1
+MESH = pl.DeviceIdType.MESH
+T_CHUNKS = 2
+P_CHUNKS = 2
 
 
 def broadcast(value, axis, source):
@@ -42,9 +49,215 @@
     return lax.psum_scatter(signed, "col", scatter_dimension=1, tiled=True)
 
 
+def kernel(pattern_ref, t_ref, l_ref, out_ref, pat, t, m, acc, p_send, p_recv,
+           load_sem, z_send, c_send, f_send, t_send, t_recv, q_send, q_recv, m_recv):
+    row = lax.axis_index("row")
+    col = lax.axis_index("col")
+    z, y = row // 2, row % 2
+    x, k = col // 2, col % 2
+    home = z % 2
+    is_home = k == home
+    rel = (k + home) % 2
+    near = (z // 2 + x) % 2
+    far = 1 - near
+    half = B // 2
+
+    def at(z_, y_, x_, k_):
+        return (z_ * 2 + y_, x_ * 2 + k_)
+
+    def slot(rel_, zrel_, y_, part=None):
+        sem = ((rel_ * 2 + zrel_) * 2 + y_) * 2
+        if part is None:
+            return m.at[rel_, zrel_, y_], m_recv.at[sem]
+        return m.at[rel_, zrel_, y_, pl.ds(part * half, half)], m_recv.at[sem + part]
+
+    def copy(src, dst, send, recv, where):
+        return pltpu.make_async_remote_copy(
+            src_ref=src, dst_ref=dst, send_sem=send, recv_sem=recv, device_id=where, device_id_type=MESH
+        )
+
+    x_mate = at(z, y, 1 - x, k)
+    sibling = at(z, y, x, 1 - k)
+    y_mate = at(z, 1 - y, x, k)
+    z_next = z + 1 - 2 * (z % 2)
+
+    barrier = pltpu.get_barrier_semaphore()
+
+    def greet(where):
+        pl.semaphore_signal(barrier, inc=1, device_id=where, device_id_type=MESH)
+
+    z_far = 2 * (1 - z // 2) + k
+    greet(at(z_far, y, x, 0))
+    greet(at(z_far, y, x, 1))
+    greet(x_mate)
+    greet(y_mate)
+    greet(sibling)
+
+    @pl.when(is_home)
+    def _():
+        greet(at(z, 1 - y, x, 1 - k))
+
+    @pl.when(jnp.logical_not(is_home))
+    def _():
+        for y_ in range(2):
+            for k_ in range(2):
+                greet(at(z_next, y_, x, k_))
+
+    load_t = pltpu.make_async_copy(t_ref, t.at[0], load_sem.at[0])
+    load_pattern = pltpu.make_async_copy(pattern_ref, pat, load_sem.at[1])
+    load_l = pltpu.make_async_copy(l_ref, m.at[0, near, y], load_sem.at[2])
+    load_pattern.start()
+    load_t.start()
+
+    @pl.when(is_home)
+    def _():
+        load_l.start()
+        pl.semaphore_wait(barrier, 7)
+
+    @pl.when(jnp.logical_not(is_home))
+    def _():
+        pl.semaphore_wait(barrier, 8)
+
+    z_copies = []
+    for part in range(2):
+        for i, z_to in enumerate((3 - z, (z + 2) % 4)):
+            dst, sem = slot(rel, near, y, part)
+            z_copies.append(copy(l_ref.at[pl.ds(part * half, half)], dst, z_send.at[part * 2 + i], sem,
+                                 at(z_to, y, x, home)))
+    mine, mine_sem = slot(rel, near, y)
+    cross = copy(l_ref, mine, c_send.at[0], mine_sem, at(z, 1 - y, x, home))
+    inside = copy(l_ref, mine, c_send.at[1], mine_sem, sibling)
+    direct = copy(l_ref, mine, c_send.at[2], mine_sem, at(z_next, y, x, home))
+    diagonal = copy(l_ref, mine, c_send.at[3], mine_sem, at(z_next, 1 - y, x, home))
+    t_rows = t.shape[1] // T_CHUNKS
+    t_copies = [
+        copy(t_ref.at[pl.ds(i * t_rows, t_rows)], t.at[1, pl.ds(i * t_rows, t_rows)],
+             t_send.at[i], t_recv.at[i], x_mate)
+        for i in range(T_CHUNKS)
+    ]
+    z_copies[0].start()
+    z_copies[1].start()
+    t_copies[0].start()
+    cross.start()
+    z_copies[2].start()
+    z_copies[3].start()
+    for c in t_copies[1:]:
+        c.start()
+    direct.start()
+    diagonal.start()
+
+    @pl.when(jnp.logical_not(is_home))
+    def _():
+        inside.start()
+
+    forwards = []
+    for part in range(2):
+        for r in range(2):
+            block, sem = slot(r, far, y, part)
+            f = copy(block, block, f_send.at[part * 2 + r], sem, y_mate)
+            f.wait_recv()
+            f.start()
+            forwards.append(f)
+
+    @pl.when(is_home)
+    def _():
+        load_l.wait()
+
+    def arrive(*place):
+        block, sem = slot(*place)
+        copy(block, block, f_send.at[0], sem, y_mate).wait_recv()
+
+    @pl.when(jnp.logical_not(is_home))
+    def _():
+        arrive(0, near, y)
+
+    arrive(1, near, y)
+    arrive(0, near, 1 - y)
+    arrive(1, near, 1 - y)
+    load_pattern.wait()
+
+    def masked(zrel):
+        plane = 2 * ((zrel + x) % 2) + k
+        blocks = []
+        for y_ in range(2):
+            keep = pat[x, plane * 2 + y_].astype(jnp.float32).astype(jnp.bfloat16)
+            blocks.append(jnp.concatenate([m[0, zrel, y_], m[1, zrel, y_]], axis=1) * keep)
+        return jnp.concatenate(blocks, axis=0)
+
+    load_t.wait()
+    for c in t_copies:
+        c.wait_recv()
+    acc[...] = jnp.dot(t[near], masked(near), preferred_element_type=jnp.float32)
+    for part in range(2):
+        for r in range(2):
+            arrive(r, far, 1 - y, part)
+    far_m = masked(far)
+    width = out_ref.shape[1]
+    p_rows = out_ref.shape[0] // P_CHUNKS
+    swaps = []
+    for i in range(P_CHUNKS):
+        rows = pl.ds(i * p_rows, p_rows)
+        total = acc[rows, :] + jnp.dot(t[far, rows, :], far_m, preferred_element_type=jnp.float32)
+        p_send[rows, :] = total[:, width:]
+        s = copy(p_send.at[rows], p_recv.at[rows], q_send.at[i], q_recv.at[i], sibling)
+        s.start()
+        swaps.append(s)
+        out_ref[rows, :] = total[:, :width]
+
+    for c in z_copies + [cross, direct, diagonal] + t_copies + forwards:
+        c.wait_send()
+
+    @pl.when(jnp.logical_not(is_home))
+    def _():
+        inside.wait_send()
+
+    negated = -pat[x, row].astype(jnp.float32)
+    for i in range(P_CHUNKS):
+        rows = pl.ds(i * p_rows, p_rows)
+        swaps[i].wait_recv()
+        out_ref[rows, :] = (out_ref[rows, :] + p_recv[rows, :]) * negated
+    for s in swaps:
+        s.wait_send()
+
+
+def fused(trailing_inverse, l_panel, pattern):
+    rows, depth = trailing_inverse.shape
+    width = l_panel.shape[1]
+    return pl.pallas_call(
+        kernel,
+        out_shape=jax.ShapeDtypeStruct((rows, width), jnp.float32),
+        in_specs=[pl.BlockSpec(memory_space=pltpu.HBM)] * 3,
+        out_specs=pl.BlockSpec(memory_space=pltpu.VMEM),
+        scratch_shapes=[
+            pltpu.SMEM(pattern.shape[::-1], jnp.int32),
+            pltpu.VMEM((2, rows, depth), jnp.bfloat16),
+            pltpu.VMEM((2, 2, 2, B, width), jnp.bfloat16),
+            pltpu.VMEM((rows, 2 * width), jnp.float32),
+            pltpu.VMEM((rows, width), jnp.float32),
+            pltpu.VMEM((rows, width), jnp.float32),
+            pltpu.SemaphoreType.DMA((3,)),
+            pltpu.SemaphoreType.DMA((4,)),
+            pltpu.SemaphoreType.DMA((4,)),
+            pltpu.SemaphoreType.DMA((4,)),
+            pltpu.SemaphoreType.DMA((T_CHUNKS,)),
+            pltpu.SemaphoreType.DMA((T_CHUNKS,)),
+            pltpu.SemaphoreType.DMA((P_CHUNKS,)),
+            pltpu.SemaphoreType.DMA((P_CHUNKS,)),
+            pltpu.SemaphoreType.DMA((16,)),
+        ],
+        compiler_params=pltpu.CompilerParams(
+            collective_id=0, has_side_effects=True, vmem_limit_bytes=66846720
+        ),
+        cost_estimate=pl.CostEstimate(
+            flops=2 * rows * 2 * depth * 2 * width, bytes_accessed=rows * depth * 4, transcendentals=0
+        ),
+    )(pattern.T, trailing_inverse, l_panel)
+
+
 def solution(mesh):
+    whole_block = (mesh.shape["row"], mesh.shape["col"]) == (8, 4)
     return jax.shard_map(
-        per_device,
+        fused if whole_block else per_device,
         mesh=mesh,
         in_specs=(P("row", "col"), P("row", "col"), P()),
         out_specs=P("row", "col"),

time: 122 us -> 20.2 us (0.17)
  waiting for transfers between devices: 95.2 us -> 0 us
  Pallas kernels: 0 us -> 18.5 us
  between operations: 13.4 us -> 0.01 us
  blocking collectives: 7.41 us -> 0 us
  matrix products: 2.17 us -> 0 us
    psum x1 -> x0, waiting for transfers between devices: 73.8 us -> none  [broadcast(): return lax.psum(kept, axis)]
    reduce_scatter x1 -> x0, waiting for transfers between devices: 21.3 us -> none  [per_device(): return lax.psum_scatter(signed, 'col', scatter_dimension=1, tiled=True)]
    pallas_call x0 -> x1, Pallas kernels: none -> 18.5 us  [fused(): pl.pallas_call(kernel, out_shape=jax.ShapeDtypeStruct((rows, width), jnp....]
    all_gather x1 -> x0, blocking collectives: 7.41 us -> none  [per_device(): full_row = lax.all_gather(l_panel, 'col', axis=1, tiled=True)]
    dot_general x1 -> x0, matrix products: 2.17 us -> none  [per_device(): jnp.dot(stacked_inverse, stacked_panel, preferred_element_type=jnp.float32)]
    reduce_scatter x1 -> x0, local copies, waits for them, and re-layouts: 1.66 us -> none  [per_device(): return lax.psum_scatter(signed, 'col', scatter_dimension=1, tiled=True)]
  transfers between devices with their start and end apart: 2 -> 0, of which waited for: 2 -> 0; matrix products, arithmetic and copies ran while one was open for 0% -> 0% of each run, Pallas kernels for 0% -> 0%
where the time goes in v2:
time: 20.2 us; the launch traced here: 20.1 us
  Pallas kernels  18.5 us (92%)
  local copies, waits for them, and re-layouts  1.57 us (8%)
    pallas_call x1, Pallas kernels, fused(): pl.pallas_call(kernel, out_shape=jax.ShapeDtypeStruct((rows, width), jnp....  18.5 us
    unnamed x1, local copies, waits for them, and re-layouts  1.57 us

profile of v2, /device:TPU:0, one launch (start us, length us, event | category | flops | bytes accessed | tf_op | source)
XLA Modules:
  0.0 20.1 jit_solution(10211423330160892783)
XLA Ops:
  0.0 18.5 %shard_map.37 = f32[256,128]{1,0:T(8,128)} custom-call(s32[2,8]{1,0:T(2,128)} %bitcast.1, bf16[256,512]{1,0:T(8,128)(2,1)} %t_ref.1, bf16[256,128]{1,0:T(8,128)(2,1)} %l_ref.1), custom_call_target="tpu_custom_call" | custom-call | flops 134217728 | bytes 524288 | tf_op jit(solution)/shard_map/pallas_call | solution.py:226
  18.5 1.6 %copy.5 = f32[256,128]{1,0:T(8,128)} copy(f32[256,128]{1,0:T(8,128)} %shard_map.37) | data formatting | bytes 262144

commit v3 on v0

--- a/solution.py
+++ b/solution.py
@@ -1,10 +1,16 @@
+import functools
+
 import jax
 import jax.numpy as jnp
 from jax import lax
+from jax.experimental import pallas as pl
+from jax.experimental.pallas import tpu as pltpu
 from jax.sharding import PartitionSpec as P
 
 B = 256
 RB = 1
+MESH = pl.DeviceIdType.MESH
+T_CHUNKS = 4
 
 
 def broadcast(value, axis, source):
@@ -42,9 +48,175 @@
     return lax.psum_scatter(signed, "col", scatter_dimension=1, tiled=True)
 
 
+def kernel(pattern_ref, t_ref, l_ref, out_ref, pat, t, m, acc,
+           load_sem, z_send, c_send, f_send, t_send, t_recv, s_send, s_recv, o_send, o_recv, m_recv):
+    row = lax.axis_index("row")
+    col = lax.axis_index("col")
+    z, y = row // 2, row % 2
+    x, k = col // 2, col % 2
+    near = (z // 2 + x) % 2
+    far = 1 - near
+    core = (z + k) % 2
+    half = B // 2
+    z_next = z + 1 - 2 * (z % 2)
+
+    def at(z_, y_, x_, k_):
+        return (z_ * 2 + y_, x_ * 2 + k_)
+
+    def slot(core_, side, y_, part=None):
+        plane = core_ * 2 + side
+        sem = (plane * 2 + y_) * 2
+        if part is None:
+            return m.at[plane, y_], m_recv.at[sem]
+        return m.at[plane, y_, pl.ds(part * half, half)], m_recv.at[sem + part]
+
+    def copy(src, dst, send, recv, where):
+        return pltpu.make_async_remote_copy(
+            src_ref=src, dst_ref=dst, send_sem=send, recv_sem=recv, device_id=where, device_id_type=MESH
+        )
+
+    x_mate = at(z, y, 1 - x, k)
+    sibling = at(z, y, x, 1 - k)
+    y_mate = at(z, 1 - y, x, k)
+    z_far = (at(3 - z, y, x, k), at((z + 2) % 4, y, x, k))
+    z_near = (at(z_next, y, x, k), at(z_next, 1 - y, x, k))
+
+    barrier = pltpu.get_barrier_semaphore()
+    mates = (*z_far, x_mate, y_mate, *z_near, sibling)
+    for where in mates:
+        pl.semaphore_signal(barrier, inc=1, device_id=where, device_id_type=MESH)
+
+    load_pattern = pltpu.make_async_copy(pattern_ref, pat, load_sem.at[0])
+    load_l = pltpu.make_async_copy(l_ref, m.at[core * 2 + near, y], load_sem.at[1])
+    load_t = pltpu.make_async_copy(t_ref, t.at[0], load_sem.at[2])
+    load_pattern.start()
+    load_l.start()
+    load_t.start()
+    pl.semaphore_wait(barrier, len(mates))
+
+    z_copies = []
+    for part in range(2):
+        for i, where in enumerate(z_far):
+            dst, sem = slot(core, near, y, part)
+            z_copies.append(copy(l_ref.at[pl.ds(part * half, half)], dst, z_send.at[part * 2 + i], sem, where))
+    mine, mine_sem = slot(core, near, y)
+    cross = copy(l_ref, mine, c_send.at[0], mine_sem, y_mate)
+    direct = copy(l_ref, mine, c_send.at[1], mine_sem, z_near[0])
+    diagonal = copy(l_ref, mine, c_send.at[2], mine_sem, z_near[1])
+    t_rows = t.shape[1] // T_CHUNKS
+    t_copies = []
+    t_forwards = []
+    for i in range(T_CHUNKS):
+        rows = pl.ds(i * t_rows, t_rows)
+        t_copies.append(copy(t_ref.at[rows], t.at[1, rows], t_send.at[i], t_recv.at[i], x_mate))
+        t_forwards.append(copy(t.at[1, rows], t.at[3, rows], s_send.at[i], s_recv.at[i], sibling))
+    t_sibling = copy(t_ref, t.at[2], o_send.at[0], o_recv.at[0], sibling)
+
+    z_copies[0].start()
+    z_copies[1].start()
+    t_copies[0].start()
+    cross.start()
+    z_copies[2].start()
+    z_copies[3].start()
+    for c in t_copies[1:]:
+        c.start()
+    direct.start()
+    diagonal.start()
+    t_sibling.start()
+
+    forwards = []
+
+    def pass_panel(part):
+        for i in range(2):
+            block, sem = slot((core + 1 + i) % 2, far, y, part)
+            f = copy(block, block, f_send.at[part * 2 + i], sem, y_mate)
+            f.wait_recv()
+            f.start()
+            forwards.append(f)
+
+    def pass_inverse(i):
+        t_copies[i].wait_recv()
+        t_forwards[i].start()
+
+    pass_inverse(0)
+    pass_panel(0)
+    for i in range(1, T_CHUNKS - 1):
+        pass_inverse(i)
+    pass_panel(1)
+    pass_inverse(T_CHUNKS - 1)
+
+    def arrive(*place):
+        block, sem = slot(*place)
+        copy(block, block, f_send.at[0], sem, y_mate).wait_recv()
+
+    def product(core_, side, y_):
+        plane = core_ * 2 + side
+        block_row = (2 * ((side + x) % 2) + (core_ + k) % 2) * 2 + y_
+        keep = pat[x, block_row].astype(jnp.float32).astype(jnp.bfloat16)
+        columns = pl.ds(pl.multiple_of(y_ * B, B), B)
+        return jnp.dot(t[plane, :, columns], m[plane, y_] * keep, preferred_element_type=jnp.float32)
+
+    load_pattern.wait()
+    load_l.wait()
+    load_t.wait()
+    t_sibling.wait_recv()
+    arrive(core, near, 1 - y)
+    arrive(1 - core, near, y)
+    arrive(1 - core, near, 1 - y)
+    for f in t_forwards:
+        f.wait_recv()
+    acc[...] = (product(0, near, 0) + product(0, near, 1) + product(1, near, 0) + product(1, near, 1)
+                + product(0, far, y) + product(1, far, y))
+    for part in range(2):
+        for i in range(2):
+            arrive(i, far, 1 - y, part)
+    negated = -pat[x, row].astype(jnp.float32)
+    out_ref[...] = (acc[...] + product(0, far, 1 - y) + product(1, far, 1 - y)) * negated
+
+    for c in z_copies + [cross, direct, diagonal, t_sibling] + t_copies + t_forwards + forwards:
+        c.wait_send()
+
+
+def fused(trailing_inverse, l_panel, pattern):
+    rows, depth = trailing_inverse.shape
+    width = l_panel.shape[1]
+    dma = pltpu.SemaphoreType.DMA
+    operands = [pltpu.with_memory_space_constraint(v, pltpu.HBM) for v in (pattern.T, trailing_inverse, l_panel)]
+    return pl.pallas_call(
+        kernel,
+        out_shape=jax.ShapeDtypeStruct((rows, width), jnp.float32),
+        in_specs=[pl.BlockSpec(memory_space=pltpu.HBM)] * 3,
+        out_specs=pl.BlockSpec(memory_space=pltpu.VMEM),
+        scratch_shapes=[
+            pltpu.SMEM(pattern.shape[::-1], jnp.int32),
+            pltpu.VMEM((4, rows, depth), jnp.bfloat16),
+            pltpu.VMEM((4, 2, B, width), jnp.bfloat16),
+            pltpu.VMEM((rows, width), jnp.float32),
+            dma((3,)),
+            dma((4,)),
+            dma((3,)),
+            dma((4,)),
+            dma((T_CHUNKS,)),
+            dma((T_CHUNKS,)),
+            dma((T_CHUNKS,)),
+            dma((T_CHUNKS,)),
+            dma((1,)),
+            dma((1,)),
+            dma((16,)),
+        ],
+        compiler_params=pltpu.CompilerParams(
+            collective_id=0, has_side_effects=True, vmem_limit_bytes=16 * 1024 * 1024
+        ),
+        cost_estimate=pl.CostEstimate(
+            flops=2 * rows * 4 * depth * width, bytes_accessed=rows * depth * 4, transcendentals=0
+        ),
+    )(*operands)
+
+
 def solution(mesh):
+    whole_block = (mesh.shape["row"], mesh.shape["col"]) == (8, 4)
     return jax.shard_map(
-        per_device,
+        fused if whole_block else per_device,
         mesh=mesh,
         in_specs=(P("row", "col"), P("row", "col"), P()),
         out_specs=P("row", "col"),

time: 122 us -> 17.3 us (0.14)
  waiting for transfers between devices: 95.2 us -> 0 us
  Pallas kernels: 0 us -> 16.5 us
  between operations: 13.4 us -> 0.01 us
  blocking collectives: 7.41 us -> 0 us
  matrix products: 2.17 us -> 0 us
  local copies, waits for them, and re-layouts: 2.54 us -> 0.66 us
    psum x1 -> x0, waiting for transfers between devices: 73.8 us -> none  [broadcast(): return lax.psum(kept, axis)]
    reduce_scatter x1 -> x0, waiting for transfers between devices: 21.3 us -> none  [per_device(): return lax.psum_scatter(signed, 'col', scatter_dimension=1, tiled=True)]
    pallas_call x0 -> x1, Pallas kernels: none -> 16.5 us  [fused(): pl.pallas_call(kernel, out_shape=jax.ShapeDtypeStruct((rows, width), jnp....]
    all_gather x1 -> x0, blocking collectives: 7.41 us -> none  [per_device(): full_row = lax.all_gather(l_panel, 'col', axis=1, tiled=True)]
    dot_general x1 -> x0, matrix products: 2.17 us -> none  [per_device(): jnp.dot(stacked_inverse, stacked_panel, preferred_element_type=jnp.float32)]
    reduce_scatter x1 -> x0, local copies, waits for them, and re-layouts: 1.66 us -> none  [per_device(): return lax.psum_scatter(signed, 'col', scatter_dimension=1, tiled=True)]
  transfers between devices with their start and end apart: 2 -> 0, of which waited for: 2 -> 0; matrix products, arithmetic and copies ran while one was open for 0% -> 0% of each run, Pallas kernels for 0% -> 0%
where the time goes in v3:
time: 17.3 us; the launch traced here: 17.2 us
  Pallas kernels  16.5 us (95%)
  local copies, waits for them, and re-layouts  0.66 us (4%)
    pallas_call x1, Pallas kernels, fused(): pl.pallas_call(kernel, out_shape=jax.ShapeDtypeStruct((rows, width), jnp....  16.5 us
    unnamed x1, local copies, waits for them, and re-layouts  0.66 us

profile of v3, /device:TPU:0, one launch (start us, length us, event | category | flops | bytes accessed | tf_op | source)
XLA Modules:
  0.0 17.2 jit_solution(5410593929989044435)
XLA Ops:
  0.0 16.5 %shard_map.37 = f32[256,128]{1,0:T(8,128)S(1)} custom-call(s32[2,8]{1,0:T(2,128)} %bitcast.1, bf16[256,512]{1,0:T(8,128)(2,1)} %t_ref.1, bf16[256,128]{1,0:T(8,128)(2,1)} %l_ref.1), custom_call_target="tpu_custom_call" | custom-call | flops 134217728 | bytes 524288 | tf_op jit(solution)/shard_map/pallas_call | solution.py:185
  16.5 0.7 %copy.5 = f32[256,128]{1,0:T(8,128)} copy(f32[256,128]{1,0:T(8,128)S(1)} %shard_map.37) | data formatting | bytes 262144

commit v4 on v3

--- a/solution.py
+++ b/solution.py
@@ -49,7 +49,8 @@
 
 
 def kernel(pattern_ref, t_ref, l_ref, out_ref, pat, t, m, acc,
-           load_sem, z_send, c_send, f_send, t_send, t_recv, s_send, s_recv, o_send, o_recv, m_recv):
+           load_sem, z_send, c_send, f_send, t_send, t_recv, s_send, s_recv, o_send, o_recv, m_recv,
+           far_sem):
     row = lax.axis_index("row")
     col = lax.axis_index("col")
     z, y = row // 2, row % 2
@@ -78,13 +79,22 @@
     x_mate = at(z, y, 1 - x, k)
     sibling = at(z, y, x, 1 - k)
     y_mate = at(z, 1 - y, x, k)
-    z_far = (at(3 - z, y, x, k), at((z + 2) % 4, y, x, k))
+    z_far = at((z + 2) % 4, y, x, k)
     z_near = (at(z_next, y, x, k), at(z_next, 1 - y, x, k))
+    early = z < 2
 
     barrier = pltpu.get_barrier_semaphore()
-    mates = (*z_far, x_mate, y_mate, *z_near, sibling)
+    mates = (y_mate, *z_near, x_mate, sibling)
+
+    def greet(sem, where):
+        pl.semaphore_signal(sem, inc=1, device_id=where, device_id_type=MESH)
+
+    @pl.when(early)
+    def _():
+        greet(barrier, z_far)
+
     for where in mates:
-        pl.semaphore_signal(barrier, inc=1, device_id=where, device_id_type=MESH)
+        greet(barrier, where)
 
     load_pattern = pltpu.make_async_copy(pattern_ref, pat, load_sem.at[0])
     load_l = pltpu.make_async_copy(l_ref, m.at[core * 2 + near, y], load_sem.at[1])
@@ -92,13 +102,10 @@
     load_pattern.start()
     load_l.start()
     load_t.start()
-    pl.semaphore_wait(barrier, len(mates))
-
     z_copies = []
     for part in range(2):
-        for i, where in enumerate(z_far):
-            dst, sem = slot(core, near, y, part)
-            z_copies.append(copy(l_ref.at[pl.ds(part * half, half)], dst, z_send.at[part * 2 + i], sem, where))
+        dst, sem = slot(core, near, y, part)
+        z_copies.append(copy(l_ref.at[pl.ds(part * half, half)], dst, z_send.at[part], sem, z_far))
     mine, mine_sem = slot(core, near, y)
     cross = copy(l_ref, mine, c_send.at[0], mine_sem, y_mate)
     direct = copy(l_ref, mine, c_send.at[1], mine_sem, z_near[0])
@@ -112,25 +119,38 @@
         t_forwards.append(copy(t.at[1, rows], t.at[3, rows], s_send.at[i], s_recv.at[i], sibling))
     t_sibling = copy(t_ref, t.at[2], o_send.at[0], o_recv.at[0], sibling)
 
-    z_copies[0].start()
-    z_copies[1].start()
+    @pl.when(early)
+    def _():
+        pl.semaphore_wait(barrier, len(mates))
+
+    @pl.when(jnp.logical_not(early))
+    def _():
+        pl.semaphore_wait(barrier, len(mates) + 1)
+        greet(far_sem, z_far)
+        for c in z_copies:
+            c.start()
+
+    cross.start()
     t_copies[0].start()
-    cross.start()
-    z_copies[2].start()
-    z_copies[3].start()
+    direct.start()
+    diagonal.start()
     for c in t_copies[1:]:
         c.start()
-    direct.start()
-    diagonal.start()
     t_sibling.start()
 
+    @pl.when(early)
+    def _():
+        pl.semaphore_wait(far_sem, 1)
+        for c in z_copies:
+            c.start()
+
     forwards = []
 
     def pass_panel(part):
-        for i in range(2):
-            block, sem = slot((core + 1 + i) % 2, far, y, part)
-            f = copy(block, block, f_send.at[part * 2 + i], sem, y_mate)
-            f.wait_recv()
+        block, sem = slot(core, far, y, part)
+        copy(block, block, f_send.at[0], sem, z_far).wait_recv()
+        for i, where in enumerate((z_near[1], y_mate, z_near[0])):
+            f = copy(block, block, f_send.at[part * 3 + i], sem, where)
             f.start()
             forwards.append(f)
 
@@ -140,10 +160,10 @@
 
     pass_inverse(0)
     pass_panel(0)
-    for i in range(1, T_CHUNKS - 1):
+    pass_inverse(1)
+    pass_panel(1)
+    for i in range(2, T_CHUNKS):
         pass_inverse(i)
-    pass_panel(1)
-    pass_inverse(T_CHUNKS - 1)
 
     def arrive(*place):
         block, sem = slot(*place)
@@ -166,12 +186,15 @@
     for f in t_forwards:
         f.wait_recv()
     acc[...] = (product(0, near, 0) + product(0, near, 1) + product(1, near, 0) + product(1, near, 1)
-                + product(0, far, y) + product(1, far, y))
+                + product(core, far, y))
     for part in range(2):
-        for i in range(2):
-            arrive(i, far, 1 - y, part)
+        arrive(core, far, 1 - y, part)
+        arrive(1 - core, far, y, part)
+    acc[...] += product(core, far, 1 - y) + product(1 - core, far, y)
+    for part in range(2):
+        arrive(1 - core, far, 1 - y, part)
     negated = -pat[x, row].astype(jnp.float32)
-    out_ref[...] = (acc[...] + product(0, far, 1 - y) + product(1, far, 1 - y)) * negated
+    out_ref[...] = (acc[...] + product(1 - core, far, 1 - y)) * negated
 
     for c in z_copies + [cross, direct, diagonal, t_sibling] + t_copies + t_forwards + forwards:
         c.wait_send()
@@ -193,9 +216,9 @@
             pltpu.VMEM((4, 2, B, width), jnp.bfloat16),
             pltpu.VMEM((rows, width), jnp.float32),
             dma((3,)),
-            dma((4,)),
+            dma((2,)),
             dma((3,)),
-            dma((4,)),
+            dma((6,)),
             dma((T_CHUNKS,)),
             dma((T_CHUNKS,)),
             dma((T_CHUNKS,)),
@@ -203,6 +226,7 @@
             dma((1,)),
             dma((1,)),
             dma((16,)),
+            pltpu.SemaphoreType.REGULAR,
         ],
         compiler_params=pltpu.CompilerParams(
             collective_id=0, has_side_effects=True, vmem_limit_bytes=16 * 1024 * 1024

time: 17.3 us -> 14.6 us (0.84)
  Pallas kernels: 16.5 us -> 13.8 us
    pallas_call x1, Pallas kernels: 16.5 us -> 13.8 us  [fused(): pl.pallas_call(kernel, out_shape=jax.ShapeDtypeStruct((rows, width), jnp....]
where the time goes in v4:
time: 14.6 us; the launch traced here: 14.5 us
  Pallas kernels  13.8 us (95%)
  local copies, waits for them, and re-layouts  0.66 us (5%)
    pallas_call x1, Pallas kernels, fused(): pl.pallas_call(kernel, out_shape=jax.ShapeDtypeStruct((rows, width), jnp....  13.8 us
    unnamed x1, local copies, waits for them, and re-layouts  0.66 us

profile of v4, /device:TPU:0, one launch (start us, length us, event | category | flops | bytes accessed | tf_op | source)
XLA Modules:
  0.0 14.5 jit_solution(2903229330181854393)
XLA Ops:
  0.0 13.8 %shard_map.37 = f32[256,128]{1,0:T(8,128)S(1)} custom-call(s32[2,8]{1,0:T(2,128)} %bitcast.1, bf16[256,512]{1,0:T(8,128)(2,1)} %t_ref.1, bf16[256,128]{1,0:T(8,128)(2,1)} %l_ref.1), custom_call_target="tpu_custom_call" | custom-call | flops 134217728 | bytes 524288 | tf_op jit(solution)/shard_map/pallas_call | solution.py:208
  13.8 0.7 %copy.5 = f32[256,128]{1,0:T(8,128)} copy(f32[256,128]{1,0:T(8,128)S(1)} %shard_map.37) | data formatting | bytes 262144

commit v5 on v4

--- a/solution.py
+++ b/solution.py
@@ -50,7 +50,7 @@
 
 def kernel(pattern_ref, t_ref, l_ref, out_ref, pat, t, m, acc,
            load_sem, z_send, c_send, f_send, t_send, t_recv, s_send, s_recv, o_send, o_recv, m_recv,
-           far_sem):
+           ready):
     row = lax.axis_index("row")
     col = lax.axis_index("col")
     z, y = row // 2, row % 2
@@ -81,20 +81,19 @@
     y_mate = at(z, 1 - y, x, k)
     z_far = at((z + 2) % 4, y, x, k)
     z_near = (at(z_next, y, x, k), at(z_next, 1 - y, x, k))
-    early = z < 2
 
     barrier = pltpu.get_barrier_semaphore()
-    mates = (y_mate, *z_near, x_mate, sibling)
+    mates = (z_far, y_mate, x_mate, z_near[0], z_near[1], sibling)
+    is_later = (z < 2, y == 0, x == 0, z % 2 == 0, z % 2 == 0, k == 1)
+    n_earlier = z // 2 + y + x + 2 * (z % 2) + 1 - k
 
     def greet(sem, where):
         pl.semaphore_signal(sem, inc=1, device_id=where, device_id_type=MESH)
 
-    @pl.when(early)
-    def _():
-        greet(barrier, z_far)
-
-    for where in mates:
-        greet(barrier, where)
+    for where, later in zip(mates, is_later):
+        @pl.when(later)
+        def _(where=where):
+            greet(barrier, where)
 
     load_pattern = pltpu.make_async_copy(pattern_ref, pat, load_sem.at[0])
     load_l = pltpu.make_async_copy(l_ref, m.at[core * 2 + near, y], load_sem.at[1])
@@ -119,30 +118,24 @@
         t_forwards.append(copy(t.at[1, rows], t.at[3, rows], s_send.at[i], s_recv.at[i], sibling))
     t_sibling = copy(t_ref, t.at[2], o_send.at[0], o_recv.at[0], sibling)
 
-    @pl.when(early)
+    @pl.when(n_earlier > 0)
     def _():
-        pl.semaphore_wait(barrier, len(mates))
-
-    @pl.when(jnp.logical_not(early))
-    def _():
-        pl.semaphore_wait(barrier, len(mates) + 1)
-        greet(far_sem, z_far)
-        for c in z_copies:
-            c.start()
-
-    cross.start()
-    t_copies[0].start()
-    direct.start()
-    diagonal.start()
-    for c in t_copies[1:]:
-        c.start()
-    t_sibling.start()
-
-    @pl.when(early)
-    def _():
-        pl.semaphore_wait(far_sem, 1)
-        for c in z_copies:
-            c.start()
+        pl.semaphore_wait(barrier, n_earlier)
+
+    groups = (z_copies, [cross], t_copies, [direct], [diagonal], [t_sibling])
+    for i, (where, later) in enumerate(zip(mates, is_later)):
+        @pl.when(jnp.logical_not(later))
+        def _(i=i, where=where):
+            greet(ready.at[i], where)
+            for c in groups[i]:
+                c.start()
+
+    for i in (1, 2, 3, 4, 0, 5):
+        @pl.when(is_later[i])
+        def _(i=i):
+            pl.semaphore_wait(ready.at[i], 1)
+            for c in groups[i]:
+                c.start()
 
     forwards = []
 
@@ -226,7 +219,7 @@
             dma((1,)),
             dma((1,)),
             dma((16,)),
-            pltpu.SemaphoreType.REGULAR,
+            pltpu.SemaphoreType.REGULAR((6,)),
         ],
         compiler_params=pltpu.CompilerParams(
             collective_id=0, has_side_effects=True, vmem_limit_bytes=16 * 1024 * 1024

time: 14.6 us -> 14.5 us (level)
  no operation moved by 1% of the time
where the time goes in v5:
time: 14.5 us; the launch traced here: 14.4 us
  Pallas kernels  13.7 us (94%)
  local copies, waits for them, and re-layouts  0.66 us (5%)
    pallas_call x1, Pallas kernels, fused(): pl.pallas_call(kernel, out_shape=jax.ShapeDtypeStruct((rows, width), jnp....  13.7 us
    unnamed x1, local copies, waits for them, and re-layouts  0.66 us

profile of v5, /device:TPU:0, one launch (start us, length us, event | category | flops | bytes accessed | tf_op | source)
XLA Modules:
  0.0 14.4 jit_solution(15912633870707319075)
XLA Ops:
  0.0 13.7 %shard_map.37 = f32[256,128]{1,0:T(8,128)S(1)} custom-call(s32[2,8]{1,0:T(2,128)} %bitcast.1, bf16[256,512]{1,0:T(8,128)(2,1)} %t_ref.1, bf16[256,128]{1,0:T(8,128)(2,1)} %l_ref.1), custom_call_target="tpu_custom_call" | custom-call | flops 134217728 | bytes 524288 | tf_op jit(solution)/shard_map/pallas_call | solution.py:201
  13.7 0.7 %copy.5 = f32[256,128]{1,0:T(8,128)} copy(f32[256,128]{1,0:T(8,128)S(1)} %shard_map.37) | data formatting | bytes 262144

commit v6 on v5

--- a/solution.py
+++ b/solution.py
@@ -151,12 +151,8 @@
         t_copies[i].wait_recv()
         t_forwards[i].start()
 
-    pass_inverse(0)
     pass_panel(0)
-    pass_inverse(1)
     pass_panel(1)
-    for i in range(2, T_CHUNKS):
-        pass_inverse(i)
 
     def arrive(*place):
         block, sem = slot(*place)
@@ -169,17 +165,31 @@
         columns = pl.ds(pl.multiple_of(y_ * B, B), B)
         return jnp.dot(t[plane, :, columns], m[plane, y_] * keep, preferred_element_type=jnp.float32)
 
+    def near_product(side):
+        return product(0, side, 0) + product(0, side, 1) + product(1, side, 0) + product(1, side, 1)
+
     load_pattern.wait()
     load_l.wait()
     load_t.wait()
-    t_sibling.wait_recv()
     arrive(core, near, 1 - y)
     arrive(1 - core, near, y)
     arrive(1 - core, near, 1 - y)
+    t_sibling.wait_recv()
+
+    @pl.when(near == 0)
+    def _():
+        acc[...] = near_product(0)
+
+    for i in range(T_CHUNKS):
+        pass_inverse(i)
     for f in t_forwards:
         f.wait_recv()
-    acc[...] = (product(0, near, 0) + product(0, near, 1) + product(1, near, 0) + product(1, near, 1)
-                + product(core, far, y))
+
+    @pl.when(near == 1)
+    def _():
+        acc[...] = near_product(1)
+
+    acc[...] += product(core, far, y)
     for part in range(2):
         arrive(core, far, 1 - y, part)
         arrive(1 - core, far, y, part)

time: 14.5 us -> 14.2 us (0.979)
  Pallas kernels: 13.7 us -> 13.4 us
    pallas_call x1, Pallas kernels: 13.7 us -> 13.4 us  [fused(): pl.pallas_call(kernel, out_shape=jax.ShapeDtypeStruct((rows, width), jnp....]
where the time goes in v6:
time: 14.2 us; the launch traced here: 14.1 us
  Pallas kernels  13.4 us (94%)
  local copies, waits for them, and re-layouts  0.66 us (5%)
    pallas_call x1, Pallas kernels, fused(): pl.pallas_call(kernel, out_shape=jax.ShapeDtypeStruct((rows, width), jnp....  13.4 us
    unnamed x1, local copies, waits for them, and re-layouts  0.66 us

profile of v6, /device:TPU:0, one launch (start us, length us, event | category | flops | bytes accessed | tf_op | source)
XLA Modules:
  0.0 14.1 jit_solution(16351274325729584476)
XLA Ops:
  0.0 13.4 %shard_map.37 = f32[256,128]{1,0:T(8,128)S(1)} custom-call(s32[2,8]{1,0:T(2,128)} %bitcast.1, bf16[256,512]{1,0:T(8,128)(2,1)} %t_ref.1, bf16[256,128]{1,0:T(8,128)(2,1)} %l_ref.1), custom_call_target="tpu_custom_call" | custom-call | flops 134217728 | bytes 524288 | tf_op jit(solution)/shard_map/pallas_call | solution.py:211
  13.4 0.7 %copy.5 = f32[256,128]{1,0:T(8,128)} copy(f32[256,128]{1,0:T(8,128)S(1)} %shard_map.37) | data formatting | bytes 262144

commit v7 on v6

--- a/solution.py
+++ b/solution.py
@@ -80,12 +80,12 @@
     sibling = at(z, y, x, 1 - k)
     y_mate = at(z, 1 - y, x, k)
     z_far = at((z + 2) % 4, y, x, k)
-    z_near = (at(z_next, y, x, k), at(z_next, 1 - y, x, k))
+    z_near = at(z_next, y, x, k)
 
     barrier = pltpu.get_barrier_semaphore()
-    mates = (z_far, y_mate, x_mate, z_near[0], z_near[1], sibling)
-    is_later = (z < 2, y == 0, x == 0, z % 2 == 0, z % 2 == 0, k == 1)
-    n_earlier = z // 2 + y + x + 2 * (z % 2) + 1 - k
+    mates = (z_far, y_mate, x_mate, z_near, sibling)
+    is_later = (z < 2, y == 0, x == 0, z % 2 == 0, k == 1)
+    n_earlier = z // 2 + y + x + z % 2 + 1 - k
 
     def greet(sem, where):
         pl.semaphore_signal(sem, inc=1, device_id=where, device_id_type=MESH)
@@ -107,8 +107,7 @@
         z_copies.append(copy(l_ref.at[pl.ds(part * half, half)], dst, z_send.at[part], sem, z_far))
     mine, mine_sem = slot(core, near, y)
     cross = copy(l_ref, mine, c_send.at[0], mine_sem, y_mate)
-    direct = copy(l_ref, mine, c_send.at[1], mine_sem, z_near[0])
-    diagonal = copy(l_ref, mine, c_send.at[2], mine_sem, z_near[1])
+    direct = copy(l_ref, mine, c_send.at[1], mine_sem, z_near)
     t_rows = t.shape[1] // T_CHUNKS
     t_copies = []
     t_forwards = []
@@ -122,7 +121,7 @@
     def _():
         pl.semaphore_wait(barrier, n_earlier)
 
-    groups = (z_copies, [cross], t_copies, [direct], [diagonal], [t_sibling])
+    groups = (z_copies, [cross], t_copies, [direct], [t_sibling])
     for i, (where, later) in enumerate(zip(mates, is_later)):
         @pl.when(jnp.logical_not(later))
         def _(i=i, where=where):
@@ -130,7 +129,7 @@
             for c in groups[i]:
                 c.start()
 
-    for i in (1, 2, 3, 4, 0, 5):
+    for i in (1, 2, 3, 0, 4):
         @pl.when(is_later[i])
         def _(i=i):
             pl.semaphore_wait(ready.at[i], 1)
@@ -139,20 +138,17 @@
 
     forwards = []
 
-    def pass_panel(part):
-        block, sem = slot(core, far, y, part)
-        copy(block, block, f_send.at[0], sem, z_far).wait_recv()
-        for i, where in enumerate((z_near[1], y_mate, z_near[0])):
-            f = copy(block, block, f_send.at[part * 3 + i], sem, where)
+    def pass_on(place, *targets):
+        block, sem = slot(*place)
+        copy(block, block, f_send.at[0], sem, y_mate).wait_recv()
+        for where in targets:
+            f = copy(block, block, f_send.at[len(forwards)], sem, where)
             f.start()
             forwards.append(f)
 
     def pass_inverse(i):
         t_copies[i].wait_recv()
         t_forwards[i].start()
-
-    pass_panel(0)
-    pass_panel(1)
 
     def arrive(*place):
         block, sem = slot(*place)
@@ -168,11 +164,14 @@
     def near_product(side):
         return product(0, side, 0) + product(0, side, 1) + product(1, side, 0) + product(1, side, 1)
 
+    pass_on((1 - core, near, y), y_mate)
+    for part in range(2):
+        pass_on((core, far, y, part), z_near, y_mate)
+
     load_pattern.wait()
     load_l.wait()
     load_t.wait()
     arrive(core, near, 1 - y)
-    arrive(1 - core, near, y)
     arrive(1 - core, near, 1 - y)
     t_sibling.wait_recv()
 
@@ -180,7 +179,11 @@
     def _():
         acc[...] = near_product(0)
 
-    for i in range(T_CHUNKS):
+    pass_on((1 - core, far, y, 0), y_mate)
+    pass_inverse(0)
+    pass_inverse(1)
+    pass_on((1 - core, far, y, 1), y_mate)
+    for i in range(2, T_CHUNKS):
         pass_inverse(i)
     for f in t_forwards:
         f.wait_recv()
@@ -189,17 +192,16 @@
     def _():
         acc[...] = near_product(1)
 
-    acc[...] += product(core, far, y)
+    acc[...] += product(core, far, y) + product(1 - core, far, y)
     for part in range(2):
         arrive(core, far, 1 - y, part)
-        arrive(1 - core, far, y, part)
-    acc[...] += product(core, far, 1 - y) + product(1 - core, far, y)
+    acc[...] += product(core, far, 1 - y)
     for part in range(2):
         arrive(1 - core, far, 1 - y, part)
     negated = -pat[x, row].astype(jnp.float32)
     out_ref[...] = (acc[...] + product(1 - core, far, 1 - y)) * negated
 
-    for c in z_copies + [cross, direct, diagonal, t_sibling] + t_copies + t_forwards + forwards:
+    for c in z_copies + [cross, direct, t_sibling] + t_copies + t_forwards + forwards:
         c.wait_send()
 
 
@@ -220,8 +222,8 @@
             pltpu.VMEM((rows, width), jnp.float32),
             dma((3,)),
             dma((2,)),
-            dma((3,)),
-            dma((6,)),
+            dma((2,)),
+            dma((7,)),
             dma((T_CHUNKS,)),
             dma((T_CHUNKS,)),
             dma((T_CHUNKS,)),
@@ -229,7 +231,7 @@
             dma((1,)),
             dma((1,)),
             dma((16,)),
-            pltpu.SemaphoreType.REGULAR((6,)),
+            pltpu.SemaphoreType.REGULAR((5,)),
         ],
         compiler_params=pltpu.CompilerParams(
             collective_id=0, has_side_effects=True, vmem_limit_bytes=16 * 1024 * 1024

time: 14.2 us -> 15.7 us (1.11)
  Pallas kernels: 13.4 us -> 14.8 us
    pallas_call x1, Pallas kernels: 13.4 us -> 14.8 us  [fused(): pl.pallas_call(kernel, out_shape=jax.ShapeDtypeStruct((rows, width), jnp....]
where the time goes in v7:
time: 15.7 us; the launch traced here: 15.5 us
  Pallas kernels  14.8 us (94%)
  local copies, waits for them, and re-layouts  0.66 us (4%)
    pallas_call x1, Pallas kernels, fused(): pl.pallas_call(kernel, out_shape=jax.ShapeDtypeStruct((rows, width), jnp....  14.8 us
    unnamed x1, local copies, waits for them, and re-layouts  0.66 us

profile of v7, /device:TPU:0, one launch (start us, length us, event | category | flops | bytes accessed | tf_op | source)
XLA Modules:
  0.0 15.5 jit_solution(16476741534841918635)
XLA Ops:
  0.0 14.8 %shard_map.37 = f32[256,128]{1,0:T(8,128)S(1)} custom-call(s32[2,8]{1,0:T(2,128)} %bitcast.1, bf16[256,512]{1,0:T(8,128)(2,1)} %t_ref.1, bf16[256,128]{1,0:T(8,128)(2,1)} %l_ref.1), custom_call_target="tpu_custom_call" | custom-call | flops 134217728 | bytes 524288 | tf_op jit(solution)/shard_map/pallas_call | solution.py:213
  14.9 0.7 %copy.5 = f32[256,128]{1,0:T(8,128)} copy(f32[256,128]{1,0:T(8,128)S(1)} %shard_map.37) | data formatting | bytes 262144

commit v8 on v6

--- a/solution.py
+++ b/solution.py
@@ -83,8 +83,8 @@
     z_near = (at(z_next, y, x, k), at(z_next, 1 - y, x, k))
 
     barrier = pltpu.get_barrier_semaphore()
-    mates = (z_far, y_mate, x_mate, z_near[0], z_near[1], sibling)
-    is_later = (z < 2, y == 0, x == 0, z % 2 == 0, z % 2 == 0, k == 1)
+    mates = (z_far, y_mate, z_near[0], z_near[1], x_mate, sibling)
+    is_later = (z < 2, y == 0, z % 2 == 0, z % 2 == 0, x == 0, k == 1)
     n_earlier = z // 2 + y + x + 2 * (z % 2) + 1 - k
 
     def greet(sem, where):
@@ -122,7 +122,7 @@
     def _():
         pl.semaphore_wait(barrier, n_earlier)
 
-    groups = (z_copies, [cross], t_copies, [direct], [diagonal], [t_sibling])
+    groups = (z_copies, [cross], [direct], [diagonal], t_copies, [t_sibling])
     for i, (where, later) in enumerate(zip(mates, is_later)):
         @pl.when(jnp.logical_not(later))
         def _(i=i, where=where):

time: 14.2 us -> 14.2 us (level)
  no operation moved by 1% of the time
where the time goes in v8:
time: 14.2 us; the launch traced here: 14 us
  Pallas kernels  13.4 us (94%)
  local copies, waits for them, and re-layouts  0.66 us (5%)
    pallas_call x1, Pallas kernels, fused(): pl.pallas_call(kernel, out_shape=jax.ShapeDtypeStruct((rows, width), jnp....  13.4 us
    unnamed x1, local copies, waits for them, and re-layouts  0.66 us

profile of v8, /device:TPU:0, one launch (start us, length us, event | category | flops | bytes accessed | tf_op | source)
XLA Modules:
  0.0 14.0 jit_solution(16955042786698835781)
XLA Ops:
  0.0 13.4 %shard_map.37 = f32[256,128]{1,0:T(8,128)S(1)} custom-call(s32[2,8]{1,0:T(2,128)} %bitcast.1, bf16[256,512]{1,0:T(8,128)(2,1)} %t_ref.1, bf16[256,128]{1,0:T(8,128)(2,1)} %l_ref.1), custom_call_target="tpu_custom_call" | custom-call | flops 134217728 | bytes 524288 | tf_op jit(solution)/shard_map/pallas_call | solution.py:211
  13.4 0.7 %copy.5 = f32[256,128]{1,0:T(8,128)} copy(f32[256,128]{1,0:T(8,128)S(1)} %shard_map.37) | data formatting | bytes 262144

commit v9 on v8

--- a/solution.py
+++ b/solution.py
@@ -108,7 +108,8 @@
     mine, mine_sem = slot(core, near, y)
     cross = copy(l_ref, mine, c_send.at[0], mine_sem, y_mate)
     direct = copy(l_ref, mine, c_send.at[1], mine_sem, z_near[0])
-    diagonal = copy(l_ref, mine, c_send.at[2], mine_sem, z_near[1])
+    passed, passed_sem = slot(1 - core, near, y)
+    relay = copy(passed, passed, c_send.at[2], passed_sem, y_mate)
     t_rows = t.shape[1] // T_CHUNKS
     t_copies = []
     t_forwards = []
@@ -122,7 +123,7 @@
     def _():
         pl.semaphore_wait(barrier, n_earlier)
 
-    groups = (z_copies, [cross], [direct], [diagonal], t_copies, [t_sibling])
+    groups = (z_copies, [cross], [direct], [], t_copies, [t_sibling])
     for i, (where, later) in enumerate(zip(mates, is_later)):
         @pl.when(jnp.logical_not(later))
         def _(i=i, where=where):
@@ -152,6 +153,8 @@
         t_forwards[i].start()
 
     pass_panel(0)
+    relay.wait_recv()
+    relay.start()
     pass_panel(1)
 
     def arrive(*place):
@@ -172,7 +175,6 @@
     load_l.wait()
     load_t.wait()
     arrive(core, near, 1 - y)
-    arrive(1 - core, near, y)
     arrive(1 - core, near, 1 - y)
     t_sibling.wait_recv()
 
@@ -199,7 +201,7 @@
     negated = -pat[x, row].astype(jnp.float32)
     out_ref[...] = (acc[...] + product(1 - core, far, 1 - y)) * negated
 
-    for c in z_copies + [cross, direct, diagonal, t_sibling] + t_copies + t_forwards + forwards:
+    for c in z_copies + [cross, direct, relay, t_sibling] + t_copies + t_forwards + forwards:
         c.wait_send()
 
 

time: 14.2 us -> 15.1 us (1.063)
  the two profiles are of different devices: /device:TPU:0 before, /device:TPU:1 now
where the time goes in v9:
time: 15.1 us; the launch traced here: 14.9 us
  Pallas kernels  14.2 us (94%)
  local copies, waits for them, and re-layouts  0.66 us (4%)
    pallas_call x1, Pallas kernels, fused(): pl.pallas_call(kernel, out_shape=jax.ShapeDtypeStruct((rows, width), jnp....  14.2 us
    unnamed x1, local copies, waits for them, and re-layouts  0.66 us

profile of v9, /device:TPU:1, one launch (start us, length us, event | category | flops | bytes accessed | tf_op | source)
XLA Modules:
  0.0 14.9 jit_solution(11285030029157859564)
XLA Ops:
  0.0 14.2 %shard_map.37 = f32[256,128]{1,0:T(8,128)S(1)} custom-call(s32[2,8]{1,0:T(2,128)} %bitcast.1, bf16[256,512]{1,0:T(8,128)(2,1)} %t_ref.1, bf16[256,128]{1,0:T(8,128)(2,1)} %l_ref.1), custom_call_target="tpu_custom_call" | custom-call | flops 134217728 | bytes 524288 | tf_op jit(solution)/shard_map/pallas_call | solution.py:213
  14.3 0.7 %copy.5 = f32[256,128]{1,0:T(8,128)} copy(f32[256,128]{1,0:T(8,128)S(1)} %shard_map.37) | data formatting | bytes 262144

commit v10 on v8

--- a/solution.py
+++ b/solution.py
@@ -11,6 +11,7 @@
 RB = 1
 MESH = pl.DeviceIdType.MESH
 T_CHUNKS = 4
+PARTS = 4
 
 
 def broadcast(value, axis, source):
@@ -58,7 +59,7 @@
     near = (z // 2 + x) % 2
     far = 1 - near
     core = (z + k) % 2
-    half = B // 2
+    piece = B // PARTS
     z_next = z + 1 - 2 * (z % 2)
 
     def at(z_, y_, x_, k_):
@@ -66,10 +67,10 @@
 
     def slot(core_, side, y_, part=None):
         plane = core_ * 2 + side
-        sem = (plane * 2 + y_) * 2
+        sem = (plane * 2 + y_) * PARTS
         if part is None:
             return m.at[plane, y_], m_recv.at[sem]
-        return m.at[plane, y_, pl.ds(part * half, half)], m_recv.at[sem + part]
+        return m.at[plane, y_, pl.ds(part * piece, piece)], m_recv.at[sem + part]
 
     def copy(src, dst, send, recv, where):
         return pltpu.make_async_remote_copy(
@@ -102,9 +103,9 @@
     load_l.start()
     load_t.start()
     z_copies = []
-    for part in range(2):
+    for part in range(PARTS):
         dst, sem = slot(core, near, y, part)
-        z_copies.append(copy(l_ref.at[pl.ds(part * half, half)], dst, z_send.at[part], sem, z_far))
+        z_copies.append(copy(l_ref.at[pl.ds(part * piece, piece)], dst, z_send.at[part], sem, z_far))
     mine, mine_sem = slot(core, near, y)
     cross = copy(l_ref, mine, c_send.at[0], mine_sem, y_mate)
     direct = copy(l_ref, mine, c_send.at[1], mine_sem, z_near[0])
@@ -151,8 +152,8 @@
         t_copies[i].wait_recv()
         t_forwards[i].start()
 
-    pass_panel(0)
-    pass_panel(1)
+    for part in range(PARTS):
+        pass_panel(part)
 
     def arrive(*place):
         block, sem = slot(*place)
@@ -190,11 +191,11 @@
         acc[...] = near_product(1)
 
     acc[...] += product(core, far, y)
-    for part in range(2):
+    for part in range(PARTS):
         arrive(core, far, 1 - y, part)
         arrive(1 - core, far, y, part)
     acc[...] += product(core, far, 1 - y) + product(1 - core, far, y)
-    for part in range(2):
+    for part in range(PARTS):
         arrive(1 - core, far, 1 - y, part)
     negated = -pat[x, row].astype(jnp.float32)
     out_ref[...] = (acc[...] + product(1 - core, far, 1 - y)) * negated
@@ -219,16 +220,16 @@
             pltpu.VMEM((4, 2, B, width), jnp.bfloat16),
             pltpu.VMEM((rows, width), jnp.float32),
             dma((3,)),
-            dma((2,)),
+            dma((PARTS,)),
             dma((3,)),
-            dma((6,)),
+            dma((3 * PARTS,)),
             dma((T_CHUNKS,)),
             dma((T_CHUNKS,)),
             dma((T_CHUNKS,)),
             dma((T_CHUNKS,)),
             dma((1,)),
             dma((1,)),
-            dma((16,)),
+            dma((8 * PARTS,)),
             pltpu.SemaphoreType.REGULAR((6,)),
         ],
         compiler_params=pltpu.CompilerParams(

time: 14.2 us -> 14.1 us (level)
  no operation moved by 1% of the time
where the time goes in v10:
time: 14.1 us; the launch traced here: 13.9 us
  Pallas kernels  13.3 us (94%)
  local copies, waits for them, and re-layouts  0.66 us (5%)
    pallas_call x1, Pallas kernels, fused(): pl.pallas_call(kernel, out_shape=jax.ShapeDtypeStruct((rows, width), jnp....  13.3 us
    unnamed x1, local copies, waits for them, and re-layouts  0.66 us

profile of v10, /device:TPU:0, one launch (start us, length us, event | category | flops | bytes accessed | tf_op | source)
XLA Modules:
  0.0 13.9 jit_solution(15630572626273087567)
XLA Ops:
  0.0 13.3 %shard_map.37 = f32[256,128]{1,0:T(8,128)S(1)} custom-call(s32[2,8]{1,0:T(2,128)} %bitcast.1, bf16[256,512]{1,0:T(8,128)(2,1)} %t_ref.1, bf16[256,128]{1,0:T(8,128)(2,1)} %l_ref.1), custom_call_target="tpu_custom_call" | custom-call | flops 134217728 | bytes 524288 | tf_op jit(solution)/shard_map/pallas_call | solution.py:212
  13.3 0.7 %copy.5 = f32[256,128]{1,0:T(8,128)} copy(f32[256,128]{1,0:T(8,128)S(1)} %shard_map.37) | data formatting | bytes 262144

commit v11 on v10

--- a/solution.py
+++ b/solution.py
@@ -128,15 +128,40 @@
         @pl.when(jnp.logical_not(later))
         def _(i=i, where=where):
             greet(ready.at[i], where)
+            if i not in (2, 3):
+                for c in groups[i]:
+                    c.start()
+
+    def start_later(*which):
+        for i in which:
+            @pl.when(is_later[i])
+            def _(i=i):
+                pl.semaphore_wait(ready.at[i], 1)
+                for c in groups[i]:
+                    c.start()
+
+    def start_near():
+        for i in (2, 3):
+            @pl.when(is_later[i])
+            def _(i=i):
+                pl.semaphore_wait(ready.at[i], 1)
+
             for c in groups[i]:
                 c.start()
 
-    for i in (1, 2, 3, 4, 0, 5):
-        @pl.when(is_later[i])
-        def _(i=i):
-            pl.semaphore_wait(ready.at[i], 1)
-            for c in groups[i]:
-                c.start()
+    start_later(1)
+
+    @pl.when(z < 2)
+    def _():
+        start_near()
+
+    start_later(4, 0, 5)
+
+    @pl.when(z >= 2)
+    def _():
+        for c in z_copies:
+            c.wait_send()
+        start_near()
 
     forwards = []
 
@@ -200,7 +225,12 @@
     negated = -pat[x, row].astype(jnp.float32)
     out_ref[...] = (acc[...] + product(1 - core, far, 1 - y)) * negated
 
-    for c in z_copies + [cross, direct, diagonal, t_sibling] + t_copies + t_forwards + forwards:
+    @pl.when(z < 2)
+    def _():
+        for c in z_copies:
+            c.wait_send()
+
+    for c in [cross, direct, diagonal, t_sibling] + t_copies + t_forwards + forwards:
         c.wait_send()
 
 

time: 14.1 us -> 14.1 us (level)
  no operation moved by 1% of the time
where the time goes in v11:
time: 14.1 us; the launch traced here: 13.9 us
  Pallas kernels  13.2 us (94%)
  local copies, waits for them, and re-layouts  0.66 us (5%)
    pallas_call x1, Pallas kernels, fused(): pl.pallas_call(kernel, out_shape=jax.ShapeDtypeStruct((rows, width), jnp....  13.2 us
    unnamed x1, local copies, waits for them, and re-layouts  0.66 us

profile of v11, /device:TPU:0, one launch (start us, length us, event | category | flops | bytes accessed | tf_op | source)
XLA Modules:
  0.0 13.9 jit_solution(8176786165001513720)
XLA Ops:
  0.0 13.2 %shard_map.37 = f32[256,128]{1,0:T(8,128)S(1)} custom-call(s32[2,8]{1,0:T(2,128)} %bitcast.1, bf16[256,512]{1,0:T(8,128)(2,1)} %t_ref.1, bf16[256,128]{1,0:T(8,128)(2,1)} %l_ref.1), custom_call_target="tpu_custom_call" | custom-call | flops 134217728 | bytes 524288 | tf_op jit(solution)/shard_map/pallas_call | solution.py:242
  13.2 0.7 %copy.5 = f32[256,128]{1,0:T(8,128)} copy(f32[256,128]{1,0:T(8,128)S(1)} %shard_map.37) | data formatting | bytes 262144

commit v12 on v10

--- a/solution.py
+++ b/solution.py
@@ -10,7 +10,7 @@
 B = 256
 RB = 1
 MESH = pl.DeviceIdType.MESH
-T_CHUNKS = 4
+T_CHUNKS = 2
 PARTS = 4
 
 

time: 14.1 us -> 14 us (level)
  no operation moved by 1% of the time
where the time goes in v12:
time: 14 us; the launch traced here: 13.8 us
  Pallas kernels  13.2 us (94%)
  local copies, waits for them, and re-layouts  0.66 us (5%)
    pallas_call x1, Pallas kernels, fused(): pl.pallas_call(kernel, out_shape=jax.ShapeDtypeStruct((rows, width), jnp....  13.2 us
    unnamed x1, local copies, waits for them, and re-layouts  0.66 us

profile of v12, /device:TPU:0, one launch (start us, length us, event | category | flops | bytes accessed | tf_op | source)
XLA Modules:
  0.0 13.8 jit_solution(6699053545471379335)
XLA Ops:
  0.0 13.2 %shard_map.37 = f32[256,128]{1,0:T(8,128)S(1)} custom-call(s32[2,8]{1,0:T(2,128)} %bitcast.1, bf16[256,512]{1,0:T(8,128)(2,1)} %t_ref.1, bf16[256,128]{1,0:T(8,128)(2,1)} %l_ref.1), custom_call_target="tpu_custom_call" | custom-call | flops 134217728 | bytes 524288 | tf_op jit(solution)/shard_map/pallas_call | solution.py:212
  13.2 0.7 %copy.5 = f32[256,128]{1,0:T(8,128)} copy(f32[256,128]{1,0:T(8,128)S(1)} %shard_map.37) | data formatting | bytes 262144
